TPU v7x, 256 devices: a whole 4x4x8 slice. The times are simulated.
256 devices in a mesh: vox: 32 (over z, y), col: 8 (over x, core).
Axes of the slice: x: 4, y: 4, z: 8, core: 2. Of those that a mesh axis runs over, the one named last changes fastest.
Arguments:
- start_modes: float32 [128, 131072], P('col', 'vox'), may hold values from -48 to 48
- start_dirs: float32 [128, 131072], P('col', 'vox'), may hold values from -6 to 6
- coupling: float32 [13, 131072], P(None, ('vox', 'col')), may hold values from 0.05 to 1
- relax_class: int32 [131072], P(('vox', 'col')), may hold values from 0 to 3
- relaxivity: float32 [4], replicated, may hold values from 0.5 to 4
Outputs:
- modes: float32 [128, 131072], P('col', 'vox')
- ritz: float32 [128, 128], replicated
All inputs are finite; a program needn't handle non-finite values.
Results may differ from a plain program's by a relative error of at most 0.0003.
Values sent between devices are 32-bit elements; how exact they have to be, the bound alone decides.
A program may use at most 64 MiB of HBM per device.

v0:
```python
import math
import jax
import jax.numpy as jnp
from jax import lax
from jax.sharding import PartitionSpec as P

NX = 256
NZ = 2
HALF = 13
ITERS = 2
QSTEPS = 3
offsets = [
    (a, b, c) for a in (-1, 0, 1) for b in (-1, 0, 1) for c in (-1, 0, 1) if (a, b, c) > (0, 0, 0)
]


def from_behind(block, axis, distance):
    devices = range(lax.axis_size(axis))
    route = [(i - distance, i) for i in devices if i - distance in devices]
    return lax.ppermute(block, axis, route)


def extended_2(block, sides, width):
    for axis, dim in sides:
        count = lax.axis_size(axis)
        forward = [(i, i + 1) for i in range(count - 1)]
        backward = [(target, source) for source, target in forward]
        low = lax.ppermute(
            lax.slice_in_dim(block, block.shape[dim] - width, None, axis=dim), axis, forward
        )
        high = lax.ppermute(lax.slice_in_dim(block, 0, width, axis=dim), axis, backward)
        block = jnp.concatenate([low, block, high], axis=dim)
    return block


def matmul(left, right):
    return jnp.dot(left, right, precision=lax.Precision.HIGHEST, preferred_element_type=jnp.float32)


def lower_solve(lower, rhs):
    return lax.linalg.triangular_solve(lower, rhs, left_side=True, lower=True)


def upper_solve(lower, rhs):
    return lax.linalg.triangular_solve(lower, rhs, left_side=True, lower=True, transpose_a=True)


def symmetric(matrix):
    return 0.5 * (matrix + matrix.T)


def project_pencil(gram_a, gram_b, count):
    sym_a = symmetric(gram_a)
    scales = lax.rsqrt(jnp.diagonal(gram_b) + 1e-06)
    normed_b = scales[:, None] * gram_b * scales[None, :]
    normed_a = scales[:, None] * sym_a * scales[None, :]
    lower = jnp.linalg.cholesky(normed_b)
    half_way = lower_solve(lower, normed_a)
    reduced = lower_solve(lower, half_way.T)
    shift = 2.0 * jnp.max(jnp.sum(jnp.abs(reduced), axis=1))
    iterate = jnp.eye(gram_a.shape[0], count, dtype=jnp.float32)
    for sweep_index in range(QSTEPS):
        iterate = shift * iterate - matmul(reduced, iterate)
        factor = jnp.linalg.cholesky(matmul(iterate.T, iterate))
        iterate = lower_solve(factor, iterate.T).T
    return scales[:, None] * upper_solve(lower, iterate)


def neighbour_sum(padded, coupled):
    rows_y = padded.shape[1] - 2
    rows_z = padded.shape[2] - 2
    rows_x = padded.shape[3] - 2
    total = jnp.zeros((padded.shape[0], rows_y, rows_z, rows_x), jnp.float32)
    for which, (step_y, step_z, step_x) in enumerate(offsets):
        ahead = padded[
            :,
            1 + step_y : 1 + step_y + rows_y,
            1 + step_z : 1 + step_z + rows_z,
            1 + step_x : 1 + step_x + rows_x,
        ]
        behind = padded[
            :,
            1 - step_y : 1 - step_y + rows_y,
            1 - step_z : 1 - step_z + rows_z,
            1 - step_x : 1 - step_x + rows_x,
        ]
        here = coupled[which, 1 : 1 + rows_y, 1 : 1 + rows_z, 1 : 1 + rows_x]
        back = coupled[
            which,
            1 - step_y : 1 - step_y + rows_y,
            1 - step_z : 1 - step_z + rows_z,
            1 - step_x : 1 - step_x + rows_x,
        ]
        total = total + here[None] * ahead
        total = total + back[None] * behind
    return total


def pad_plane(array):
    return jnp.pad(array, ((0, 0), (0, 0), (1, 1), (1, 1)))


def quotient(modes, images):
    total = lax.psum(matmul(modes, images.T), ("vox", "col"))
    return symmetric(total)


def on_device(start_modes, start_dirs, coupling, relax_class, relaxivity):
    local_voxels = coupling.shape[1]
    match = relax_class[:, None] == jnp.arange(relaxivity.shape[0], dtype=jnp.int32)[None, :]
    voxel_rate = jnp.sum(jnp.where(match, relaxivity[None, :], jnp.float32(0.0)), axis=1)
    damping = 1.0 / (1.0 + voxel_rate)
    own_coupling = coupling.reshape(HALF, 1, NZ, NX)
    before = from_behind(own_coupling, ("vox", "col"), 1)
    coupled = pad_plane(
        jnp.concatenate([before, own_coupling, jnp.zeros_like(own_coupling)], axis=1)
    )
    position = lax.axis_index(("vox", "col"))
    device_count = lax.axis_size(("vox", "col"))
    plane = jnp.ones((1, 1, NZ, NX), jnp.float32)
    upper_flag = (position > 0).astype(jnp.float32)
    lower_flag = (position < device_count - 1).astype(jnp.float32)
    unity = pad_plane(jnp.concatenate([upper_flag * plane, plane, lower_flag * plane], axis=1))
    degree = neighbour_sum(unity, coupled).reshape(local_voxels)
    diagonal = degree + voxel_rate

    def operate(field):
        count = field.shape[0]
        shaped = field.reshape(count, 1, NZ, NX)
        extended = extended_2(shaped, ((("vox", "col"), 1),), 1)
        padded = pad_plane(extended)
        return diagonal[None, :] * field - neighbour_sum(padded, coupled).reshape(
            count, local_voxels
        )

    modes, dirs = (
        lax.all_to_all(start_modes, "col", split_axis=1, concat_axis=0, tiled=True),
        lax.all_to_all(start_dirs, "col", split_axis=1, concat_axis=0, tiled=True),
    )
    count = modes.shape[0]
    images = operate(modes)
    dir_images = operate(dirs)
    ritz = quotient(modes, images)
    for iteration in range(ITERS):
        resid = images - matmul(ritz, modes)
        search = resid * damping[None, :]
        search_images = operate(search)
        basis = jnp.concatenate([modes, search, dirs], axis=0)
        basis_images = jnp.concatenate([images, search_images, dir_images], axis=0)
        local_a = matmul(basis, basis_images.T)
        local_b = matmul(basis, basis.T)
        gram_a, gram_b = lax.psum((local_a, local_b), ("vox", "col"))
        coeffs = project_pencil(gram_a, gram_b, count)
        modes = matmul(coeffs.T, basis)
        images = matmul(coeffs.T, basis_images)
        dirs = matmul(coeffs[count:].T, basis[count:])
        dir_images = matmul(coeffs[count:].T, basis_images[count:])
        ritz = quotient(modes, images)
    total_voxels = device_count * local_voxels
    scaled = modes * math.sqrt(total_voxels)
    modes_out = lax.all_to_all(scaled, "col", split_axis=0, concat_axis=1, tiled=True)
    return (modes_out, ritz)


def solution(mesh):
    in_specs = (P("col", "vox"), P("col", "vox"), P(None, ("vox", "col")), P(("vox", "col")), P())
    out_specs = (P("col", "vox"), P())
    return jax.shard_map(
        on_device, mesh=mesh, in_specs=in_specs, out_specs=out_specs, check_vma=False
    )
```

profile of v0, /device:TPU:1, one launch (start us, length us, event | category | flops | bytes accessed | tf_op | source)
XLA Modules:
  0.0 1733.3 jit_solution(11976527018198322847)
XLA Ops:
  7.2 1.7 copy.120
  8.8 6.6 all-to-all-start
  16.2 3.5 collective-permute-start
  22.8 1.7 copy.119
  25.2 4.1 all-to-all-start.1
  29.5 2.0 collective-permute-start.2
  31.4 3.6 collective-permute-start.1
  36.0 2.9 collective-permute-start.6
  38.9 2.6 collective-permute-start.5
  41.6 2.3 select_maximum_fusion.6
  43.9 4.5 multiply_subtract_fusion.3
  49.6 3.4 select_maximum_fusion.2
  53.1 245.1 %all-reduce.15.cloned.1.call-done = f32[128,128]{0,1:T(8,128)} async-done(((f32[128,128]{0,1:T(8,128)}), f32[128,128]{0,1:T(8,128)}) %all-reduce.15.cloned.1.call-update) | async-done | bytes 65552 | tf_op jit(solution)/shard_map/psum | solution.py:104
  301.3 2.0 collective-permute-start.4
  303.3 3.9 collective-permute-start.3
  307.2 5.4 fusion.64
  312.7 2.2 fusion.38
  314.9 2.3 select_maximum_fusion.4
  317.3 4.4 fusion.89
  322.7 2.3 fusion.14
  325.0 256.1 %all-reduce.23.cloned.1.call-done = (f32[384,384]{1,0:T(8,128)}, f32[384,384]{0,1:T(8,128)}) async-done(((f32[384,384]{1,0:T(8,128)}, f32[384,384]{0,1:T(8,128)}), (f32[384,384]{1,0:T(8,128)}, f32[384,384]{0,1:T(8,128)})) %all-reduce.23.cloned.1.call-update) | async-done | bytes 1179664 | tf_op jit(solution)/shard_map/psum | solution.py:152
  581.2 6.6 gather_fusion
  590.4 11.7 cholesky.310
  602.2 9.8 custom-call.40
  614.4 11.7 cholesky.329
  626.2 9.9 custom-call.41
  637.5 11.7 cholesky.348
  652.6 5.9 while.12
  653.2 1.3 bitcast_dynamic-update-slice_fusion.4
  658.5 29.7 %custom-call.47 = f32[3,128,128]{1,2,0:T(8,128)S(1)} custom-call(f32[3,128,128]{2,1,0:T(8,128)S(1)} %get-tuple-element.49), custom_call_target="InvertDiagBlocksLowerTriangular" | custom-call | tf_op jit(solution)/shard_map/triangular_solve/custom-call.8 | solution.py:45
  695.7 11.7 cholesky.361
  708.7 9.8 custom-call.44
  720.8 11.7 cholesky.372
  733.9 9.8 custom-call.45
  745.5 11.9 cholesky.383
  758.7 9.8 custom-call.46
  773.6 237.5 %all-reduce.17.cloned.1.call-done = f32[128,128]{1,0:T(8,128)} async-done(((f32[128,128]{1,0:T(8,128)}), f32[128,128]{1,0:T(8,128)}) %all-reduce.17.cloned.1.call-update) | async-done | bytes 65552 | tf_op jit(solution)/shard_map/psum | solution.py:104
  1013.5 1.9 collective-permute-start.8
  1015.4 3.6 collective-permute-start.7
  1019.5 2.2 fusion.36
  1022.4 2.3 select_maximum_fusion
  1024.6 4.4 fusion.39
  1029.2 2.3 fusion.12
  1031.5 259.7 %all-reduce.21.cloned.1.call-done = (f32[384,384]{1,0:T(8,128)}, f32[384,384]{0,1:T(8,128)}) async-done(((f32[384,384]{1,0:T(8,128)}, f32[384,384]{0,1:T(8,128)}), (f32[384,384]{1,0:T(8,128)}, f32[384,384]{0,1:T(8,128)})) %all-reduce.21.cloned.1.call-update) | async-done | bytes 1179664 | tf_op jit(solution)/shard_map/psum | solution.py:152
  1291.2 6.6 gather_fusion.1
  1300.6 11.7 cholesky.396
  1312.4 9.8 custom-call.48
  1324.5 11.7 cholesky.415
  1336.3 10.2 custom-call.49
  1347.8 11.7 cholesky.434
  1363.5 6.4 while.13
  1364.2 1.4 bitcast_dynamic-update-slice_fusion.5
  1366.3 1.4 bitcast_dynamic-update-slice_fusion.5
  1368.4 1.4 bitcast_dynamic-update-slice_fusion.5
  1369.9 29.7 %custom-call.55 = f32[3,128,128]{1,2,0:T(8,128)S(1)} custom-call(f32[3,128,128]{2,1,0:T(8,128)S(1)} %get-tuple-element.52), custom_call_target="InvertDiagBlocksLowerTriangular" | custom-call | tf_op jit(solution)/shard_map/triangular_solve/custom-call.8 | solution.py:45
  1407.1 11.7 cholesky.447
  1420.1 9.8 custom-call.52
  1432.0 11.7 cholesky.458
  1445.0 9.8 custom-call.53
  1456.7 11.9 cholesky.469
  1470.0 9.8 custom-call.54
  1481.7 1.4 broadcast_multiply_fusion
  1485.0 7.1 all-to-all-start.2
  1492.1 231.0 %all-reduce.19.cloned.1.call-done = f32[128,128]{1,0:T(8,128)} async-done(((f32[128,128]{1,0:T(8,128)}), f32[128,128]{1,0:T(8,128)}) %all-reduce.19.cloned.1.call-update) | async-done | bytes 65552 | tf_op jit(solution)/shard_map/psum | solution.py:104
  (313 shorter events, 78.5 us)
Async XLA Ops:
  8.8 16.4 all-to-all-start
  16.2 8.8 collective-permute-start
  25.2 10.6 all-to-all-start.1
  29.3 268.9 %all-reduce.15.cloned.1.call-start = ((), (), s32[]{:S(2)}) async-start(), calls=%async_computation.3 | async-start | bytes 131072 | tf_op jit(solution)/shard_map/psum | solution.py:104
  29.5 12.1 collective-permute-start.2
  31.4 10.1 collective-permute-start.1
  35.1 13.3 copy-start.21
  35.1 13.3 copy-start.23
  35.1 13.3 copy-start.25
  35.1 13.3 copy-start.27
  35.2 13.3 copy-start.29
  35.2 13.3 copy-start.31
  35.2 13.3 copy-start.33
  35.8 17.2 copy-start.35
  36.0 12.5 copy-start.15
  36.0 13.6 collective-permute-start.6
  38.9 10.7 collective-permute-start.5
  49.6 531.6 %all-reduce.23.cloned.1.call-start = ((), (), s32[]{:S(2)}) async-start(), calls=%async_computation.7 | async-start | bytes 2359296 | tf_op jit(solution)/shard_map/psum | solution.py:152
  49.6 3.4 copy-start.14
  301.3 13.6 copy-start.16
  301.3 13.6 collective-permute-start.4
  303.3 11.6 collective-permute-start.3
  312.6 4.6 copy-start.22
  312.6 4.6 copy-start.24
  312.6 4.6 copy-start.26
  312.6 4.6 copy-start.28
  312.6 4.6 copy-start.30
  312.6 4.6 copy-start.32
  312.7 4.6 copy-start.34
  317.3 4.5 copy-start.36
  321.9 0.7 copy-start.6
  321.9 0.8 copy-start.8
  325.0 686.1 %all-reduce.17.cloned.1.call-start = ((), (), s32[]{:S(2)}) async-start(), calls=%async_computation.4 | async-start | bytes 131072 | tf_op jit(solution)/shard_map/psum | solution.py:104
  581.2 6.6 copy-start.2
  581.2 7.7 copy-start
  590.4 11.7 copy-start.12
  744.1 26.5 %copy-start.7 = (f32[128,512]{1,0:T(8,128)S(1)}, f32[128,512]{1,0:T(8,128)}, u32[]{:S(2)}) copy-start(f32[128,512]{1,0:T(8,128)} %copy-done.6) | copy-start | bytes 786436
  744.1 26.5 %copy-start.9 = (f32[128,512]{1,0:T(8,128)S(1)}, f32[128,512]{1,0:T(8,128)}, u32[]{:S(2)}) copy-start(f32[128,512]{1,0:T(8,128)} %copy-done.8) | copy-start | bytes 786436
  770.2 241.8 %copy-start.37 = (f32[512]{0:T(512)S(1)}, f32[512]{0:T(512)}, u32[]{:S(2)}) copy-start(f32[512]{0:T(512)} %get-tuple-element.163) | copy-start | bytes 6148
  771.3 257.8 %copy-start.4 = (f32[128,512]{1,0:T(8,128)}, f32[128,512]{1,0:T(8,128)S(1)}, u32[]{:S(2)}) copy-start(f32[128,512]{1,0:T(8,128)S(1)} %fusion.13) | copy-start | bytes 786436
  773.1 518.2 %all-reduce.21.cloned.1.call-start = ((), (), s32[]{:S(2)}) async-start(), calls=%async_computation.6 | async-start | bytes 2359296 | tf_op jit(solution)/shard_map/psum | solution.py:152
  773.6 255.6 %copy-start.10 = (f32[128,512]{1,0:T(8,128)}, f32[128,512]{1,0:T(8,128)S(1)}, u32[]{:S(2)}) copy-start(f32[128,512]{1,0:T(8,128)S(1)} %fusion.15) | copy-start | bytes 786436
  1013.5 8.3 collective-permute-start.8
  1015.4 6.9 collective-permute-start.7
  1019.5 9.7 copy-start.17
  1029.2 268.7 %copy-start.19 = (f32[128,512]{1,0:T(8,128)}, f32[128,512]{1,0:T(8,128)S(1)}, u32[]{:S(2)}) copy-start(f32[128,512]{1,0:T(8,128)S(1)} %multiply_subtract_fusion) | copy-start | bytes 786436
  1031.5 691.6 %all-reduce.19.cloned.1.call-start = ((), (), s32[]{:S(2)}) async-start(), calls=%async_computation.5 | async-start | bytes 131072 | tf_op jit(solution)/shard_map/psum | solution.py:104
  1291.2 6.7 copy-start.3
  1291.2 7.7 copy-start.1
  1300.5 11.7 copy-start.13
  1454.8 26.9 %copy-start.11 = (f32[128,512]{1,0:T(8,128)S(1)}, f32[128,512]{1,0:T(8,128)}, u32[]{:S(2)}) copy-start(f32[128,512]{1,0:T(8,128)} %copy-done.10) | copy-start | bytes 786436
  1455.9 27.2 %copy-start.5 = (f32[128,512]{1,0:T(8,128)S(1)}, f32[128,512]{1,0:T(8,128)}, u32[]{:S(2)}) copy-start(f32[128,512]{1,0:T(8,128)} %copy-done.4) | copy-start | bytes 786436
  1455.9 27.2 %copy-start.18 = (f32[128,512]{1,0:T(8,128)S(1)}, f32[128,512]{1,0:T(8,128)}, u32[]{:S(2)}) copy-start(f32[128,512]{1,0:T(8,128)} %copy-done.17) | copy-start | bytes 786436
  1455.9 27.2 %copy-start.20 = (f32[128,512]{1,0:T(8,128)S(1)}, f32[128,512]{1,0:T(8,128)}, u32[]{:S(2)}) copy-start(f32[128,512]{1,0:T(8,128)} %copy-done.19) | copy-start | bytes 786436
  1485.0 240.7 %all-to-all-start.2 = ((f32[8,16,512]{2,1,0:T(8,128)}), f32[8,16,512]{2,1,0:T(8,128)S(1)}, u32[]{:S(2)}, u32[]{:S(2)}) async-start(f32[8,16,512]{2,1,0:T(8,128)} %bitcast.87), calls=%async_computation.2 | async-start | bytes 524288 | tf_op jit(solution)/shard_map/all_to_all | solution.py:161
Sparse Core Ops, SparseCore 0:
  49.7 248.4 all-reduce.14
  325.1 256.0 all-reduce.22
  773.2 237.8 all-reduce.16
  1031.6 259.5 all-reduce.20
  1485.1 237.9 all-reduce.18
where the time goes:
time: 1740 us; the launch traced here: 1730 us
  waiting for transfers between devices  1230 us (71%)
  other arithmetic  348 us (20%)
  matrix products  48.7 us (3%)
  starting transfers between devices  44.1 us (3%)
  local copies, waits for them, and re-layouts  41.4 us (2%)
  between operations  21 us (1%)
    psum x3, waiting for transfers between devices, quotient(): total = lax.psum(matmul(modes, images.T), ('vox', 'col'))  714 us
    psum x2, waiting for transfers between devices, on_device(): gram_a, gram_b = lax.psum((local_a, local_b), ('vox', 'col'))  516 us
    another operation x21, other arithmetic, project_pencil(): lower = jnp.linalg.cholesky(normed_b)  114 us
    another operation x18, other arithmetic, project_pencil(): factor = jnp.linalg.cholesky(matmul(iterate.T, iterate))  74.7 us
    another operation x12, other arithmetic, lower_solve(): return lax.linalg.triangular_solve(lower, rhs, left_side=True, lower=True)  62.8 us
    another operation x5, other arithmetic, upper_solve(): lax.linalg.triangular_solve(lower, rhs, left_side=True, lower=True, trans...  59.5 us
  transfers between devices with their start and end apart: 17, of which 6 were waited for; matrix products, arithmetic and copies ran while one was open for 2% of the time, Pallas kernels for 0%

commit v1 on v0

--- a/solution.py
+++ b/solution.py
@@ -101,7 +101,7 @@
 
 
 def quotient(modes, images):
-    total = lax.psum(matmul(modes, images.T), ("vox", "col"))
+    total = lax.psum(lax.psum(matmul(modes, images.T), "vox"), "col")
     return symmetric(total)
 
 

time: 1740 us -> 1640 us (0.943)
  waiting for transfers between devices: 1230 us -> 1120 us
    psum x3 -> x6, waiting for transfers between devices: 714 us -> 600 us  [quotient(): total = lax.psum(lax.psum(matmul(modes, images.T), 'vox'), 'col')]
  transfers between devices with their start and end apart: 17 -> 20, of which waited for: 6 -> 9; matrix products, arithmetic and copies ran while one was open for 2% -> 2% of each run, Pallas kernels for 0% -> 0%
where the time goes in v1:
time: 1640 us; the launch traced here: 1630 us
  waiting for transfers between devices  1120 us (68%)
  other arithmetic  349 us (21%)
  matrix products  48.7 us (3%)
  starting transfers between devices  48 us (3%)
  local copies, waits for them, and re-layouts  42.1 us (3%)
  between operations  21.3 us (1%)
    psum x6, waiting for transfers between devices, quotient(): total = lax.psum(lax.psum(matmul(modes, images.T), 'vox'), 'col')  600 us
    psum x2, waiting for transfers between devices, on_device(): gram_a, gram_b = lax.psum((local_a, local_b), ('vox', 'col'))  524 us
    another operation x21, other arithmetic, project_pencil(): lower = jnp.linalg.cholesky(normed_b)  114 us
    another operation x18, other arithmetic, project_pencil(): factor = jnp.linalg.cholesky(matmul(iterate.T, iterate))  74.7 us
    another operation x12, other arithmetic, lower_solve(): return lax.linalg.triangular_solve(lower, rhs, left_side=True, lower=True)  62.8 us
    another operation x5, other arithmetic, upper_solve(): lax.linalg.triangular_solve(lower, rhs, left_side=True, lower=True, trans...  59.5 us
  transfers between devices with their start and end apart: 20, of which 9 were waited for; matrix products, arithmetic and copies ran while one was open for 2% of the time, Pallas kernels for 0%

profile of v1, /device:TPU:1, one launch (start us, length us, event | category | flops | bytes accessed | tf_op | source)
XLA Modules:
  0.0 1634.1 jit_solution(14013786607438789904)
XLA Ops:
  7.2 1.7 copy.120
  8.8 6.6 all-to-all-start
  16.2 3.5 collective-permute-start
  22.8 1.7 copy.119
  25.2 4.1 all-to-all-start.1
  29.5 2.0 collective-permute-start.2
  31.4 3.6 collective-permute-start.1
  36.0 2.9 collective-permute-start.6
  38.9 2.6 collective-permute-start.5
  41.6 2.3 select_maximum_fusion.6
  43.9 5.1 multiply_subtract_fusion.3
  50.2 3.4 select_maximum_fusion.2
  54.3 141.3 %all-reduce.18.cloned.1.call-done = f32[128,128]{0,1:T(8,128)} async-done(((f32[128,128]{0,1:T(8,128)}), f32[128,128]{0,1:T(8,128)}) %all-reduce.18.cloned.1.call-update) | async-done | bytes 65552 | tf_op jit(solution)/shard_map/psum | solution.py:104
  196.8 65.3 %all-reduce.20.cloned.1.call-done = f32[128,128]{0,1:T(8,128)} async-done(((f32[128,128]{0,1:T(8,128)}), f32[128,128]{0,1:T(8,128)}) %all-reduce.20.cloned.1.call-update) | async-done | bytes 65552 | tf_op jit(solution)/shard_map/psum | solution.py:104
  265.1 4.8 collective-permute-start.4
  269.9 2.1 collective-permute-start.3
  272.0 5.4 fusion.64
  277.5 2.2 fusion.38
  279.7 2.3 select_maximum_fusion.4
  282.1 4.4 fusion.89
  287.5 2.3 fusion.14
  289.9 260.7 %all-reduce.32.cloned.1.call-done = (f32[384,384]{1,0:T(8,128)}, f32[384,384]{0,1:T(8,128)}) async-done(((f32[384,384]{1,0:T(8,128)}, f32[384,384]{0,1:T(8,128)}), (f32[384,384]{1,0:T(8,128)}, f32[384,384]{0,1:T(8,128)})) %all-reduce.32.cloned.1.call-update) | async-done | bytes 1179664 | tf_op jit(solution)/shard_map/psum | solution.py:152
  550.6 6.6 gather_fusion
  559.8 11.7 cholesky.310
  571.6 9.8 custom-call.40
  583.8 11.7 cholesky.329
  595.6 9.9 custom-call.41
  606.8 11.7 cholesky.348
  622.0 5.9 while.12
  627.9 29.7 %custom-call.47 = f32[3,128,128]{1,2,0:T(8,128)S(1)} custom-call(f32[3,128,128]{2,1,0:T(8,128)S(1)} %get-tuple-element.49), custom_call_target="InvertDiagBlocksLowerTriangular" | custom-call | tf_op jit(solution)/shard_map/triangular_solve/custom-call.8 | solution.py:45
  665.1 11.7 cholesky.361
  678.1 9.8 custom-call.44
  690.2 11.7 cholesky.372
  703.3 9.8 custom-call.45
  714.9 11.9 cholesky.383
  728.1 9.8 custom-call.46
  742.5 134.9 %all-reduce.22.cloned.1.call-done = f32[128,128]{1,0:T(8,128)} async-done(((f32[128,128]{1,0:T(8,128)}), f32[128,128]{1,0:T(8,128)}) %all-reduce.22.cloned.1.call-update) | async-done | bytes 65552 | tf_op jit(solution)/shard_map/psum | solution.py:104
  878.0 65.6 %all-reduce.24.cloned.1.call-done = f32[128,128]{1,0:T(8,128)} async-done(((f32[128,128]{1,0:T(8,128)}), f32[128,128]{1,0:T(8,128)}) %all-reduce.24.cloned.1.call-update) | async-done | bytes 65552 | tf_op jit(solution)/shard_map/psum | solution.py:104
  946.0 4.6 collective-permute-start.8
  950.6 1.9 collective-permute-start.7
  953.0 2.2 fusion.36
  955.9 2.3 select_maximum_fusion
  958.2 4.4 fusion.39
  962.7 2.3 fusion.12
  965.0 263.4 %all-reduce.30.cloned.1.call-done = (f32[384,384]{1,0:T(8,128)}, f32[384,384]{0,1:T(8,128)}) async-done(((f32[384,384]{1,0:T(8,128)}, f32[384,384]{0,1:T(8,128)}), (f32[384,384]{1,0:T(8,128)}, f32[384,384]{0,1:T(8,128)})) %all-reduce.30.cloned.1.call-update) | async-done | bytes 1179664 | tf_op jit(solution)/shard_map/psum | solution.py:152
  1228.4 6.6 gather_fusion.1
  1237.7 11.7 cholesky.396
  1249.5 9.8 custom-call.48
  1261.7 11.7 cholesky.415
  1273.4 10.2 custom-call.49
  1285.0 11.7 cholesky.434
  1300.7 6.4 while.13
  1305.6 1.4 bitcast_dynamic-update-slice_fusion.5
  1307.0 29.7 %custom-call.55 = f32[3,128,128]{1,2,0:T(8,128)S(1)} custom-call(f32[3,128,128]{2,1,0:T(8,128)S(1)} %get-tuple-element.52), custom_call_target="InvertDiagBlocksLowerTriangular" | custom-call | tf_op jit(solution)/shard_map/triangular_solve/custom-call.8 | solution.py:45
  1344.2 11.7 cholesky.447
  1357.3 9.8 custom-call.52
  1369.1 11.7 cholesky.458
  1382.2 9.8 custom-call.53
  1393.8 11.9 cholesky.469
  1407.1 9.8 custom-call.54
  1418.9 1.4 broadcast_multiply_fusion
  1422.2 135.1 %all-reduce.26.cloned.1.call-done = f32[128,128]{1,0:T(8,128)} async-done(((f32[128,128]{1,0:T(8,128)}), f32[128,128]{1,0:T(8,128)}) %all-reduce.26.cloned.1.call-update) | async-done | bytes 65552 | tf_op jit(solution)/shard_map/psum | solution.py:104
  1557.3 9.0 all-to-all-start.2
  1566.2 57.4 %all-reduce.28.cloned.1.call-done = f32[128,128]{1,0:T(8,128)} async-done(((f32[128,128]{1,0:T(8,128)}), f32[128,128]{1,0:T(8,128)}) %all-reduce.28.cloned.1.call-update) | async-done | bytes 65552 | tf_op jit(solution)/shard_map/psum | solution.py:104
  (324 shorter events, 84.3 us)
Async XLA Ops:
  8.8 16.4 %all-to-all-start = ((f32[16,8,512]{2,0,1:T(8,128)}), f32[16,8,512]{2,0,1:T(8,128)S(1)}, u32[]{:S(2)}, u32[]{:S(2)}) async-start(f32[16,8,512]{2,0,1:T(8,128)} %bitcast.334), calls=%async_computation | async-start | bytes 524288 | tf_op jit(solution)/shard_map/all_to_all | solution.py:137
  16.2 8.8 collective-permute-start
  25.2 10.6 all-to-all-start.1
  29.3 166.4 %all-reduce.18.cloned.1.call-start = ((), (), s32[]{:S(2)}) async-start(), calls=%async_computation.3 | async-start | bytes 131072 | tf_op jit(solution)/shard_map/psum | solution.py:104
  29.5 12.1 collective-permute-start.2
  31.4 10.1 collective-permute-start.1
  35.1 13.9 copy-start.22
  35.1 13.9 copy-start.24
  35.1 13.9 copy-start.26
  35.1 13.9 copy-start.28
  35.2 13.9 copy-start.30
  35.2 13.9 copy-start.32
  35.2 13.9 copy-start.34
  35.8 160.0 %copy-start.36 = (f32[512]{0:T(512)}, f32[512]{0:T(512)S(1)}, u32[]{:S(2)}) copy-start(f32[512]{0:T(512)S(1)} %get-tuple-element.164) | copy-start | bytes 6148
  36.0 13.1 copy-start.15
  36.0 14.2 collective-permute-start.6
  38.9 11.3 collective-permute-start.5
  49.1 4.5 copy-start.16
  50.2 211.9 %all-reduce.20.cloned.1.call-start = ((), (), s32[]{:S(2)}) async-start(), calls=%async_computation.4 | async-start | bytes 131072 | tf_op jit(solution)/shard_map/psum | solution.py:104
  50.2 145.5 %copy-start.14 = (f32[128,1,2,256]{3,2,0,1:T(2,128)}, f32[128,1,2,256]{3,2,0,1:T(2,128)S(1)}, u32[]{:S(2)}) copy-start(f32[128,1,2,256]{3,2,0,1:T(2,128)S(1)} %collective-permute-done.6) | copy-start | bytes 786436
  195.7 354.9 %all-reduce.32.cloned.1.call-start = ((), (), s32[]{:S(2)}) async-start(), calls=%async_computation.10 | async-start | bytes 2359296 | tf_op jit(solution)/shard_map/psum | solution.py:152
  265.1 14.6 copy-start.17
  265.1 14.6 collective-permute-start.4
  269.9 9.9 collective-permute-start.3
  277.4 4.6 copy-start.23
  277.5 4.6 copy-start.25
  277.5 4.6 copy-start.27
  277.5 4.6 copy-start.29
  277.5 4.6 copy-start.31
  277.5 4.6 copy-start.33
  277.5 4.6 copy-start.35
  282.1 4.5 copy-start.37
  286.7 0.7 copy-start.6
  286.7 0.8 copy-start.8
  289.8 587.6 %all-reduce.22.cloned.1.call-start = ((), (), s32[]{:S(2)}) async-start(), calls=%async_computation.5 | async-start | bytes 131072 | tf_op jit(solution)/shard_map/psum | solution.py:104
  550.6 6.6 copy-start.2
  550.6 7.7 copy-start
  559.8 11.7 copy-start.12
  713.5 26.5 %copy-start.7 = (f32[128,512]{1,0:T(8,128)S(1)}, f32[128,512]{1,0:T(8,128)}, u32[]{:S(2)}) copy-start(f32[128,512]{1,0:T(8,128)} %copy-done.6) | copy-start | bytes 786436
  713.5 26.5 %copy-start.9 = (f32[128,512]{1,0:T(8,128)S(1)}, f32[128,512]{1,0:T(8,128)}, u32[]{:S(2)}) copy-start(f32[128,512]{1,0:T(8,128)} %copy-done.8) | copy-start | bytes 786436
  739.8 204.7 %copy-start.38 = (f32[512]{0:T(512)S(1)}, f32[512]{0:T(512)}, u32[]{:S(2)}) copy-start(f32[512]{0:T(512)} %get-tuple-element.163) | copy-start | bytes 6148
  740.7 222.0 %copy-start.4 = (f32[128,512]{1,0:T(8,128)}, f32[128,512]{1,0:T(8,128)S(1)}, u32[]{:S(2)}) copy-start(f32[128,512]{1,0:T(8,128)S(1)} %fusion.13) | copy-start | bytes 786436
  742.4 201.2 %all-reduce.24.cloned.1.call-start = ((), (), s32[]{:S(2)}) async-start(), calls=%async_computation.6 | async-start | bytes 131072 | tf_op jit(solution)/shard_map/psum | solution.py:104
  877.4 351.0 %all-reduce.30.cloned.1.call-start = ((), (), s32[]{:S(2)}) async-start(), calls=%async_computation.9 | async-start | bytes 2359296 | tf_op jit(solution)/shard_map/psum | solution.py:152
  878.0 84.7 %copy-start.10 = (f32[128,512]{1,0:T(8,128)}, f32[128,512]{1,0:T(8,128)S(1)}, u32[]{:S(2)}) copy-start(f32[128,512]{1,0:T(8,128)S(1)} %fusion.15) | copy-start | bytes 786436
  946.0 9.3 collective-permute-start.8
  950.6 5.2 collective-permute-start.7
  953.0 9.6 copy-start.18
  962.7 272.4 %copy-start.20 = (f32[128,512]{1,0:T(8,128)}, f32[128,512]{1,0:T(8,128)S(1)}, u32[]{:S(2)}) copy-start(f32[128,512]{1,0:T(8,128)S(1)} %multiply_subtract_fusion) | copy-start | bytes 786436
  965.0 592.3 %all-reduce.26.cloned.1.call-start = ((), (), s32[]{:S(2)}) async-start(), calls=%async_computation.7 | async-start | bytes 131072 | tf_op jit(solution)/shard_map/psum | solution.py:104
  1228.4 6.7 copy-start.3
  1228.4 7.7 copy-start.1
  1237.7 11.7 copy-start.13
  1392.0 26.9 %copy-start.11 = (f32[128,512]{1,0:T(8,128)S(1)}, f32[128,512]{1,0:T(8,128)}, u32[]{:S(2)}) copy-start(f32[128,512]{1,0:T(8,128)} %copy-done.10) | copy-start | bytes 786436
  1393.1 27.3 %copy-start.5 = (f32[128,512]{1,0:T(8,128)S(1)}, f32[128,512]{1,0:T(8,128)}, u32[]{:S(2)}) copy-start(f32[128,512]{1,0:T(8,128)} %copy-done.4) | copy-start | bytes 786436
  1393.1 27.2 %copy-start.19 = (f32[128,512]{1,0:T(8,128)S(1)}, f32[128,512]{1,0:T(8,128)}, u32[]{:S(2)}) copy-start(f32[128,512]{1,0:T(8,128)} %copy-done.18) | copy-start | bytes 786436
  1393.1 27.2 %copy-start.21 = (f32[128,512]{1,0:T(8,128)S(1)}, f32[128,512]{1,0:T(8,128)}, u32[]{:S(2)}) copy-start(f32[128,512]{1,0:T(8,128)} %copy-done.20) | copy-start | bytes 786436
  1422.1 201.5 %all-reduce.28.cloned.1.call-start = ((), (), s32[]{:S(2)}) async-start(), calls=%async_computation.8 | async-start | bytes 131072 | tf_op jit(solution)/shard_map/psum | solution.py:104
  1557.3 68.8 %all-to-all-start.2 = ((f32[8,16,512]{2,1,0:T(8,128)}), f32[8,16,512]{2,1,0:T(8,128)S(1)}, u32[]{:S(2)}, u32[]{:S(2)}) async-start(f32[8,16,512]{2,1,0:T(8,128)} %bitcast.87), calls=%async_computation.2 | async-start | bytes 524288 | tf_op jit(solution)/shard_map/all_to_all | solution.py:161
Sparse Core Ops, SparseCore 0:
  50.3 145.3 all-reduce.17
  198.0 63.9 all-reduce.19
  289.9 260.6 all-reduce.31
  742.6 134.8 all-reduce.21
  879.6 63.9 all-reduce.23
  965.1 263.2 all-reduce.29
  1422.2 134.9 all-reduce.25
  1559.6 63.9 all-reduce.27
